TPU v7x, 512 devices: a whole 4x4x16 slice. The times are simulated.
512 devices in a mesh: seq: 128 (over y, z, core), head: 4 (over x).
Axes of the slice: x: 4, y: 4, z: 16, core: 2. Of those that a mesh axis runs over, the one named last changes fastest.
Arguments:
- queries: bfloat16 [32768, 4096], P('seq', 'head'), may hold values from -6 to 6
- key_vectors: bfloat16 [32768, 4096], P('seq', 'head'), may hold values from -6 to 6
- value_vectors: bfloat16 [32768, 4096], P('seq', 'head'), may hold values from -6 to 6
- norm_gain: float32 [4096], P('head'), may hold values from 0.1 to 1.9
- out_weight: bfloat16 [4096, 4096], P('head', 'seq'), may hold values from -0.09375 to 0.09375
Outputs:
- projected: bfloat16 [32768, 4096], P('seq', 'head')
All inputs are finite; a program needn't handle non-finite values.
Results may differ from a plain program's by a relative error of at most 0.022.
Values may be sent and summed in bfloat16 or wider, within the bound.
A program may use at most 192 MiB of HBM per device.

v0:
```python
import jax
import jax.numpy as jnp
from jax import lax
from jax.sharding import PartitionSpec as P

HD = 128
BLOCK = 256


epsilon = 1e-06


def carried_in(shard, axis, join, neutral):
    place = lax.axis_index(axis)
    gathered = lax.all_gather(shard.astype(jnp.bfloat16), axis)
    state = jnp.zeros_like(shard) + jnp.asarray(neutral, shard.dtype)

    def one(hop, state):
        return join(state, lax.dynamic_index_in_dim(gathered, hop, 0, False).astype(shard.dtype))

    return lax.fori_loop(0, place, one, state)


def add_states(earlier, later):
    return earlier + later


def body(queries, key_vectors, value_vectors, norm_gain, out_weight):
    row_count = queries.shape[0]
    feature_count = queries.shape[1]
    head_count = feature_count // HD
    block_count = row_count // BLOCK
    shape_four = (block_count, BLOCK, head_count, HD)
    query_blocks = queries.reshape(shape_four)
    key_blocks = key_vectors.reshape(shape_four)
    value_blocks = value_vectors.reshape(shape_four)
    block_terms = jnp.einsum(
        "bshd,bshe->bhde", key_blocks, value_blocks, preferred_element_type=jnp.float32
    )
    inclusive = jnp.cumsum(block_terms, axis=0)
    device_total = inclusive[-1]
    empty_state = jnp.zeros((1, head_count, HD, HD), jnp.float32)
    earlier_blocks = jnp.concatenate([empty_state, inclusive[:-1]], axis=0)
    incoming = carried_in(device_total, "seq", add_states, jnp.zeros_like(device_total))
    state_in = (incoming[None] + earlier_blocks).astype(jnp.bfloat16)
    positions = jnp.arange(BLOCK, dtype=jnp.int32)
    causal = positions[:, None] >= positions[None, :]
    scores = jnp.einsum(
        "bthd,bshd->bhts", query_blocks, key_blocks, preferred_element_type=jnp.float32
    )
    scores = jnp.where(causal[None, None], scores, jnp.float32(0.0)).astype(jnp.bfloat16)
    within = jnp.einsum("bhts,bshd->bthd", scores, value_blocks, preferred_element_type=jnp.float32)
    carried = jnp.einsum(
        "bthd,bhde->bthe", query_blocks, state_in, preferred_element_type=jnp.float32
    )
    combined = within + carried
    root_mean = jnp.sqrt(jnp.mean(combined * combined, axis=-1, keepdims=True) + epsilon)
    gain_table = norm_gain.reshape(head_count, HD)
    attended = (combined / root_mean * gain_table[None, None]).astype(jnp.bfloat16)
    attended = attended.reshape(row_count, feature_count)
    full_weight = lax.all_gather(out_weight, "seq", axis=1, tiled=True)
    partial_sums = jnp.dot(attended, full_weight, preferred_element_type=jnp.float32)
    projected = lax.psum_scatter(
        partial_sums.astype(jnp.bfloat16), "head", scatter_dimension=1, tiled=True
    )
    return projected


def solution(mesh):
    in_specs = (P("seq", "head"), P("seq", "head"), P("seq", "head"), P("head"), P("head", "seq"))
    out_specs = P("seq", "head")
    return jax.shard_map(body, mesh=mesh, in_specs=in_specs, out_specs=out_specs, check_vma=False)
```

profile of v0, /device:TPU:1, one launch (start us, length us, event | category | flops | bytes accessed | tf_op | source)
XLA Modules:
  0.0 403.7 jit_solution(14020149944886877765)
XLA Ops:
  6.5 0.0 copy-start
  6.5 0.0 copy-start.1
  6.5 0.0 all-gather.6.cloned.1.call-start
  6.5 1.3 copy.17
  7.8 2.0 convolution_convert_fusion.1
  9.9 0.0 all-gather.6.cloned.1.call-update
  9.9 0.0 all-gather.4.cloned.1.call-start
  10.0 0.7 all-gather.4.cloned.1.call-update
  10.7 0.0 reduce-scatter.2.cloned.1.call-start
  10.8 200.6 %all-gather.6.cloned.1.call-done = bf16[1024,128,128]{2,1,0:T(8,128)(2,1)} async-done(((bf16[8,128,128]{2,1,0:T(8,128)(2,1)}), bf16[1024,128,128]{2,1,0:T(8,128)(2,1)}) %all-gather.6.cloned.1.call-update) | async-done | bytes 33554448 | tf_op jit(solution)/shard_map/all_gather | solution.py:15
  211.4 1.1 while.10
  211.4 1.1 convert_add_fusion.2
  212.5 0.0 copy-done
  212.5 0.4 fusion.10
  212.8 1.8 multiply_reduce_fusion
  214.7 0.0 copy-done.1
  214.7 0.2 multiply_convert_fusion
  214.9 142.9 %all-gather.4.cloned.1.call-done = bf16[1024,4096]{0,1:T(8,128)(2,1)} async-done(((bf16[1024,32]{0,1:T(8,128)(2,1)}), bf16[1024,4096]{0,1:T(8,128)(2,1)}) %all-gather.4.cloned.1.call-update) | async-done | bytes 8388624 | tf_op jit(solution)/shard_map/all_gather | solution.py:61
  357.8 7.2 %convolution_convert_fusion = bf16[256,4096]{1,0:T(8,128)(2,1)} fusion(bf16[256,1024]{0,1:T(8,128)(2,1)S(1)} %bitcast.55, bf16[1024,4096]{0,1:T(8,128)(2,1)} %all-gather.4.cloned.1.call-done), kind=kOutput, calls=%fused_computation.1 | convolution fusion | flops 2148532224 | bytes 11010048 | tf_op jit(solution)/shard_map/dot_general | solution.py:62
  365.0 0.0 reduce-scatter.2.cloned.1.call-update
  365.0 32.2 %reduce-scatter.2.cloned.1.call-done = bf16[256,1024]{1,0:T(8,128)(2,1)} async-done(((bf16[256,4096]{1,0:T(8,128)(2,1)}), bf16[256,1024]{1,0:T(8,128)(2,1)}) %reduce-scatter.2.cloned.1.call-update) | async-done | bytes 524304 | tf_op jit(solution)/shard_map/reduce_scatter | solution.py:63
  (3 shorter events, 0.1 us)
Async XLA Ops:
  6.5 205.9 %copy-start = (bf16[256,1024]{1,0:T(8,128)(2,1)S(1)}, bf16[256,1024]{1,0:T(8,128)(2,1)}, u32[]{:S(2)}) copy-start(bf16[256,1024]{1,0:T(8,128)(2,1)} %param.7) | copy-start | bytes 1572868
  6.5 208.1 %copy-start.1 = (f32[1024]{0:T(1024)S(1)}, f32[1024]{0:T(1024)}, u32[]{:S(2)}) copy-start(f32[1024]{0:T(1024)} %param.10) | copy-start | bytes 12292
  6.5 204.8 %all-gather.6.cloned.1.call-start = ((), (), s32[]{:S(2)}) async-start(), calls=%async_computation.3 | async-start | bytes 33816576 | tf_op jit(solution)/shard_map/all_gather | solution.py:15
  9.9 347.9 %all-gather.4.cloned.1.call-start = ((), (), s32[]{:S(2)}) async-start(), calls=%async_computation.1 | async-start | bytes 8454144 | tf_op jit(solution)/shard_map/all_gather | solution.py:61
  10.7 386.5 %reduce-scatter.2.cloned.1.call-start = ((), (), s32[]{:S(2)}) async-start(), calls=%async_computation.2 | async-start | bytes 2621440 | tf_op jit(solution)/shard_map/reduce_scatter | solution.py:63
Sparse Core Ops, SparseCore 0:
  10.5 200.7 all-gather.5
  214.5 143.2 all-gather.3
  365.1 32.0 reduce-scatter.1
where the time goes:
time: 408 us; the launch traced here: 404 us
  waiting for transfers between devices  376 us (92%)
  between operations  13.2 us (3%)
  matrix products  11.4 us (3%)
    all_gather x1, waiting for transfers between devices, carried_in(): gathered = lax.all_gather(shard.astype(jnp.bfloat16), axis)  201 us
    all_gather x1, waiting for transfers between devices, body(): full_weight = lax.all_gather(out_weight, 'seq', axis=1, tiled=True)  143 us
    reduce_scatter x1, waiting for transfers between devices, body(): lax.psum_scatter(partial_sums.astype(jnp.bfloat16), 'head', scatter_dimen...  32.2 us
  transfers between devices with their start and end apart: 3, of which 3 were waited for; matrix products, arithmetic and copies ran while one was open for 1% of the time, Pallas kernels for 0%

commit v1 on v0

v1 whole, which is shorter than its diff:
```python
import jax
import jax.numpy as jnp
from jax import lax
from jax.experimental import pallas as pl
from jax.experimental.pallas import tpu as pltpu
from jax.sharding import PartitionSpec as P

HD = 128
NY, NZ, NX = 4, 16, 4
EPS = 1e-06
MESH = pl.DeviceIdType.MESH
TICKS = 9
CHUNKS = 4


def slots(tick):
    if tick == 0:
        return 0, 1
    if tick == 8:
        return 15, 1
    return 2 * tick - 1, 2


def kernel(
    q_hbm, k_hbm, v_hbm, gain_hbm, w_hbm, out_ref,
    q_v, k_v, v_v, gain_v, q_t, within, gain_t, t_own, t_send, t_sib, c_send, z_in, pre, y_in,
    p_out, p_half, s_send, s_all, att, w_buf, x1_send, x1_recv, x2_send, x2_recv, keep,
    load_sem, sib_sem, once_send, once_recv, wz_recv, wl_recv, wr_recv, w2_recv, ws_recv, w_send,
    x1_sem, x2_sem, x_send,
):
    s = lax.axis_index("seq")
    x = lax.axis_index("head")
    c = lax.rem(s, 2)
    z = lax.rem(s // 2, NZ)
    y = s // (2 * NZ)

    def at(dy=0, dz=0, dx=0, flip=False):
        yy, zz = lax.rem(y + dy + NY, NY), lax.rem(z + dz + NZ, NZ)
        return ((yy * NZ + zz) * 2 + (1 - c if flip else c), lax.rem(x + dx + NX, NX))

    def remote(src, dst, send, recv, device):
        return pltpu.make_async_remote_copy(
            src_ref=src, dst_ref=dst, send_sem=send, recv_sem=recv, device_id=device, device_id_type=MESH
        )

    def take(ref, sem):
        pltpu.make_async_copy(ref, ref, sem).wait()

    z_far = [8, 7, 9, 6, 10, 5, 11, 4, 12, 3, 13, 2, 14, 1, 15]
    barrier = pltpu.get_barrier_semaphore()
    partners = [at(dz=d) for d in z_far] + [at(dy=d) for d in (1, 2, 3)] + [at(dx=1), at(dx=-1), at(flip=True)]
    for partner in partners:
        pl.semaphore_signal(barrier, inc=1, device_id=partner, device_id_type=MESH)

    loads = [
        pltpu.make_async_copy(v_hbm, v_v, load_sem.at[0]),
        pltpu.make_async_copy(k_hbm, k_v, load_sem.at[1]),
        pltpu.make_async_copy(q_hbm, q_v, load_sem.at[2]),
        pltpu.make_async_copy(gain_hbm, gain_v, load_sem.at[3]),
        pltpu.make_async_copy(w_hbm, w_buf.at[y, 0, c], load_sem.at[4]),
    ]
    for load in loads:
        load.start()
    loads[0].wait()
    loads[1].wait()

    heads = q_v.shape[1] // HD
    half = heads * HD // 2
    for h in range(heads):
        cols = pl.ds(h * HD, HD)
        v_t = v_v[:, cols].T
        state = jnp.dot(v_t, k_v[:, cols], preferred_element_type=jnp.float32)
        t_own[cols, :] = state
        t_send[cols, :] = state.astype(jnp.bfloat16)
    loads[2].wait()
    loads[3].wait()
    loads[4].wait()

    pl.semaphore_wait(barrier, len(partners))

    mine = pl.ds(pl.multiple_of(c * half, half), half)
    other = pl.ds(pl.multiple_of((1 - c) * half, half), half)
    t_copy = remote(t_send.at[other], t_sib, sib_sem.at[0], sib_sem.at[1], at(flip=True))
    t_copy.start()

    rel = [y, lax.rem(y + NY - 1, NY), lax.rem(y + 1, NY), lax.rem(y + 2, NY)]

    def w_at(row, tick):
        first, count = slots(tick)
        return w_buf.at[rel[row], pl.ds(first, count), c]

    def to_sibling(row, tick):
        part = w_at(row, tick)
        remote(part, part, w_send.at[3], ws_recv.at[tick, row], at(flip=True)).start()

    def along_z(slot_from, slot_to, dz):
        remote(
            w_buf.at[y, slot_from, c], w_buf.at[y, slot_to, c], w_send.at[0], wz_recv.at[slot_to], at(dz=dz)
        ).start()

    def tick(k):
        if k == 0:
            along_z(0, 1, 1)
            along_z(0, 2, -1)
        elif k < TICKS:
            take(w_buf.at[y, 2 * k - 1, c], wz_recv.at[2 * k - 1])
            if k < 8:
                along_z(2 * k - 1, 2 * k + 1, 1)
                take(w_buf.at[y, 2 * k, c], wz_recv.at[2 * k])
            if k < 7:
                along_z(2 * k, 2 * k + 2, -1)
        if k < TICKS:
            part = w_at(0, k)
            remote(part, part, w_send.at[1], wl_recv.at[k], at(dy=1)).start()
            remote(part, part, w_send.at[1], wr_recv.at[k], at(dy=-1)).start()
            to_sibling(0, k)
        j = k - 1
        if 0 <= j < TICKS:
            first, count = slots(j)
            take(w_at(1, j), wl_recv.at[j])
            for slot in range(first, first + count):
                if slot % 2 == 0:
                    part = w_buf.at[rel[1], slot, c]
                    remote(part, part, w_send.at[2], w2_recv.at[slot], at(dy=1)).start()
            to_sibling(1, j)
            take(w_at(2, j), wr_recv.at[j])
            for slot in range(first, first + count):
                if slot % 2 == 1:
                    part = w_buf.at[rel[2], slot, c]
                    remote(part, part, w_send.at[2], w2_recv.at[slot], at(dy=-1)).start()
            to_sibling(2, j)
        j = k - 2
        if 0 <= j < TICKS:
            first, count = slots(j)
            for slot in range(first, first + count):
                take(w_buf.at[rel[3], slot, c], w2_recv.at[slot])
            to_sibling(3, j)

    tick(0)

    t_copy.wait_recv()
    c_send[...] = (t_own[mine, :] + t_sib[...].astype(jnp.float32)).astype(jnp.bfloat16).reshape(c_send.shape)
    for d in z_far:
        remote(
            c_send.at[lax.rem(z + d, NZ)], z_in.at[z], once_send.at[0], once_recv.at[0], at(dz=d)
        ).start()
    z_in[z] = c_send[z]

    before = lax.broadcasted_iota(jnp.int32, (256, 256), 0) <= lax.broadcasted_iota(jnp.int32, (256, 256), 1)
    for h in range(heads):
        cols = pl.ds(h * HD, HD)
        q_t[cols, :] = q_v[:, cols].T
        scores = jnp.dot(k_v[:, cols], q_t[cols, :], preferred_element_type=jnp.float32)
        scores = jnp.where(before, scores, 0.0).astype(jnp.bfloat16)
        v_t = v_v[:, cols].T
        within[cols, :] = jnp.dot(v_t, scores, preferred_element_type=jnp.float32)
        gain_t[cols, :] = jnp.broadcast_to(gain_v[h : h + 1, :], (HD, HD)).T

    tick(1)
    tick(2)

    take(z_in.at[pl.ds(0, NZ - 1)], once_recv.at[0])
    total = jnp.zeros(z_in.shape[1:], jnp.float32)
    for j in range(NZ):
        pre[j] = total
        total = total + z_in[j].astype(jnp.float32)
    y_in[y] = total.astype(jnp.bfloat16)
    for d in (2, 1, 3):
        remote(y_in.at[y], y_in.at[y], once_send.at[1], once_recv.at[1], at(dy=d)).start()
    tick(3)
    take(y_in.at[pl.ds(0, NY - 1)], once_recv.at[1])
    base = jnp.zeros(z_in.shape[1:], jnp.float32)
    for j in range(NY):
        base = base + jnp.where(j < y, y_in[j].astype(jnp.float32), 0.0)
    for j in range(NZ):
        p_out[j] = (base + pre[j]).astype(jnp.bfloat16)
    for d in z_far:
        remote(
            p_out.at[lax.rem(z + d, NZ)], p_half.at[z], once_send.at[2], once_recv.at[2], at(dz=d)
        ).start()
    p_half[z] = p_out[z]
    tick(4)
    tick(5)
    take(p_half.at[pl.ds(0, NZ - 1)], once_recv.at[2])
    prefix = p_half[...].astype(jnp.float32).reshape(half, HD)
    s_send[...] = (prefix + jnp.where(c == 0, t_own[mine, :], 0.0)).astype(jnp.bfloat16)
    s_copy = remote(s_send, s_all.at[mine], sib_sem.at[2], sib_sem.at[3], at(flip=True))
    s_copy.start()
    s_all[mine, :] = (prefix + jnp.where(c == 1, t_sib[...].astype(jnp.float32), 0.0)).astype(jnp.bfloat16)
    take(s_all.at[other], sib_sem.at[3])

    for h in range(heads):
        cols = pl.ds(h * HD, HD)
        combined = within[cols, :] + jnp.dot(s_all[cols, :], q_t[cols, :], preferred_element_type=jnp.float32)
        mean = jnp.mean(combined * combined, axis=0, keepdims=True)
        att[cols, :] = (combined * lax.rsqrt(mean + EPS) * gain_t[cols, 0:1]).astype(jnp.bfloat16)

    right, left, across = lax.rem(x + 1, NX), lax.rem(x + NX - 1, NX), lax.rem(x + 2, NX)

    def partial(dest, g):
        w = w_buf[dest, 4 * g : 4 * g + 4].reshape(256, w_buf.shape[-1])
        return jnp.dot(w, att[...], preferred_element_type=jnp.float32)

    def x2_start(g, way, part, dx):
        remote(
            x2_send.at[g, way, part], x2_recv.at[g, way, part], x_send, x2_sem.at[g, way, part], at(dx=dx)
        ).start()

    def project(g):
        for t in ((0, 1, 2), (3, 4), (5, 6), (7, 8))[g]:
            for row in range(4):
                first, count = slots(t)
                take(w_buf.at[rel[row], pl.ds(first, count), 1 - c], ws_recv.at[t, row])
        far = partial(across, g).astype(jnp.bfloat16).reshape(2, 128, 256)
        for way, dx in ((0, 1), (1, -1)):
            x1_send[g, way] = far[way]
            remote(x1_send.at[g, way], x1_recv.at[g, way], x_send, x1_sem.at[g, way], at(dx=dx)).start()
        near = partial(right, g)
        x2_send[g, 0, 1] = near[128:].astype(jnp.bfloat16)
        x2_start(g, 0, 1, 1)
        keep[g, 0] = near[:128]
        near = partial(left, g)
        x2_send[g, 1, 0] = near[:128].astype(jnp.bfloat16)
        x2_start(g, 1, 0, -1)
        keep[g, 1] = near[128:]
        own = partial(x, g)
        keep[g, 2] = own[:128]
        keep[g, 3] = own[128:]

    def join(g):
        for way, dx in ((0, 1), (1, -1)):
            take(x1_recv.at[g, way], x1_sem.at[g, way])
            x2_send[g, way, way] = (keep[g, way] + x1_recv[g, way].astype(jnp.float32)).astype(jnp.bfloat16)
            x2_start(g, way, way, dx)

    def finish(g):
        for way, part in ((0, 1), (1, 0), (0, 0), (1, 1)):
            take(x2_recv.at[g, way, part], x2_sem.at[g, way, part])
        for part in range(2):
            total = keep[g, 2 + part] + (
                x2_recv[g, 0, part].astype(jnp.float32) + x2_recv[g, 1, part].astype(jnp.float32)
            )
            total = total.astype(jnp.bfloat16)
            for i in range(2):
                slot = 4 * g + 2 * part + i
                step = (slot + 1) // 2
                where = lax.rem(z + (NZ - step if slot % 2 == 1 else step), NZ)
                out_ref[pl.ds(pl.multiple_of(where * 64, 64), 64), :] = total[64 * i : 64 * i + 64]

    project(0)
    tick(6)
    project(1)
    join(0)
    tick(7)
    tick(8)
    project(2)
    join(1)
    finish(0)
    tick(9)
    tick(10)
    project(3)
    join(2)
    finish(1)
    join(3)
    finish(2)
    finish(3)

    t_copy.wait_send()
    s_copy.wait_send()
    take(z_in.at[pl.ds(0, NZ - 1)], once_send.at[0])
    take(y_in.at[pl.ds(0, NY - 1)], once_send.at[1])
    take(p_half.at[pl.ds(0, NZ - 1)], once_send.at[2])
    take(w_buf.at[0, pl.ds(0, 15), 0], w_send.at[0])
    take(w_buf.at[pl.ds(0, 2), pl.ds(0, 16), 0], w_send.at[1])
    take(w_buf.at[0, pl.ds(0, 16), 0], w_send.at[2])
    take(w_buf.at[pl.ds(0, 4), pl.ds(0, 16), 0], w_send.at[3])
    take(w_buf.at[0, pl.ds(0, 12), pl.ds(0, 2)], x_send)


def body(queries, key_vectors, value_vectors, norm_gain, out_weight):
    tokens, features = queries.shape
    heads = features // HD
    half = features // 2
    bf16, f32 = jnp.bfloat16, jnp.float32
    sem = pltpu.SemaphoreType.DMA
    anywhere = pl.BlockSpec(memory_space=pl.ANY)
    out = pl.pallas_call(
        kernel,
        out_shape=jax.ShapeDtypeStruct((features, tokens), bf16),
        in_specs=[anywhere] * 5,
        out_specs=pl.BlockSpec(memory_space=pltpu.VMEM),
        scratch_shapes=[
            pltpu.VMEM((tokens, features), bf16),
            pltpu.VMEM((tokens, features), bf16),
            pltpu.VMEM((tokens, features), bf16),
            pltpu.VMEM((heads, HD), f32),
            pltpu.VMEM((features, tokens), bf16),
            pltpu.VMEM((features, tokens), f32),
            pltpu.VMEM((features, HD), f32),
            pltpu.VMEM((features, HD), f32),
            pltpu.VMEM((features, HD), bf16),
            pltpu.VMEM((half, HD), bf16),
            pltpu.VMEM((NZ, half // NZ, HD), bf16),
            pltpu.VMEM((NZ, half // NZ, HD), bf16),
            pltpu.VMEM((NZ, half // NZ, HD), f32),
            pltpu.VMEM((NY, half // NZ, HD), bf16),
            pltpu.VMEM((NZ, half // NZ, HD), bf16),
            pltpu.VMEM((NZ, half // NZ, HD), bf16),
            pltpu.VMEM((half, HD), bf16),
            pltpu.VMEM((features, HD), bf16),
            pltpu.VMEM((features, tokens), bf16),
            pltpu.VMEM((NY, NZ, 2, 32, features), bf16),
            pltpu.VMEM((CHUNKS, 2, 128, tokens), bf16),
            pltpu.VMEM((CHUNKS, 2, 128, tokens), bf16),
            pltpu.VMEM((CHUNKS, 2, 2, 128, tokens), bf16),
            pltpu.VMEM((CHUNKS, 2, 2, 128, tokens), bf16),
            pltpu.VMEM((CHUNKS, 4, 128, tokens), f32),
            sem((5,)),
            sem((4,)),
            sem((3,)),
            sem((3,)),
            sem((16,)),
            sem((TICKS,)),
            sem((TICKS,)),
            sem((16,)),
            sem((TICKS, 4)),
            sem((4,)),
            sem((CHUNKS, 2)),
            sem((CHUNKS, 2, 2)),
            sem,
        ],
        compiler_params=pltpu.CompilerParams(
            collective_id=0, has_side_effects=True, vmem_limit_bytes=48 << 20
        ),
        cost_estimate=pl.CostEstimate(flops=2_550_000_000, bytes_accessed=12_000_000, transcendentals=4096),
        name="attend_and_project",
    )(queries, key_vectors, value_vectors, norm_gain.reshape(heads, HD), out_weight.T)
    return out.T


def solution(mesh):
    in_specs = (P("seq", "head"), P("seq", "head"), P("seq", "head"), P("head"), P("head", "seq"))
    return jax.shard_map(body, mesh=mesh, in_specs=in_specs, out_specs=P("seq", "head"), check_vma=False)
```

time: 408 us -> 81.4 us (0.20)
  waiting for transfers between devices: 376 us -> 0 us
  Pallas kernels: 0 us -> 75.4 us
  between operations: 13.2 us -> 0.01 us
  matrix products: 11.4 us -> 0 us
  local copies, waits for them, and re-layouts: 1.34 us -> 5.65 us
    all_gather x2 -> x0, waiting for transfers between devices: 344 us -> none  [the longest x1 201 us: carried_in(): gathered = lax.all_gather(shard.astype(jnp.bfloat16), axis)]
    pallas_call x0 -> x1, Pallas kernels: none -> 75.4 us  [body(): pl.pallas_call(kernel, out_shape=jax.ShapeDtypeStruct((features, tokens),...]
    reduce_scatter x1 -> x0, waiting for transfers between devices: 32.2 us -> none  [body(): lax.psum_scatter(partial_sums.astype(jnp.bfloat16), 'head', scatter_dimen...]
    dot_general x4 -> x0, matrix products: 11.4 us -> none  [the longest x1 7.19 us: body(): jnp.dot(attended, full_weight, preferred_element_type=jnp.float32)]
    unnamed x4 -> x10, local copies, waits for them, and re-layouts: 0.01 us -> 4.65 us
  transfers between devices with their start and end apart: 3 -> 0, of which waited for: 3 -> 0; matrix products, arithmetic and copies ran while one was open for 1% -> 0% of each run, Pallas kernels for 0% -> 0%
where the time goes in v1:
time: 81.4 us; the launch traced here: 81 us
  Pallas kernels  75.4 us (93%)
  local copies, waits for them, and re-layouts  5.65 us (7%)
    pallas_call x1, Pallas kernels, body(): pl.pallas_call(kernel, out_shape=jax.ShapeDtypeStruct((features, tokens),...  75.4 us
    unnamed x10, local copies, waits for them, and re-layouts  4.65 us

profile of v1, /device:TPU:1, one launch (start us, length us, event | category | flops | bytes accessed | tf_op | source)
XLA Modules:
  0.0 81.0 jit_solution(2824713877651798031)
XLA Ops:
  0.0 0.0 copy-start
  0.0 1.0 %copy-done = bf16[256,1024]{1,0:T(8,128)(2,1)S(1)} copy-done((bf16[256,1024]{1,0:T(8,128)(2,1)S(1)}, bf16[256,1024]{1,0:T(8,128)(2,1)}, u32[]{:S(2)}) %copy-start) | copy-done | bytes 524312
  1.0 0.0 copy-start.1
  1.0 1.0 %copy-done.1 = bf16[256,1024]{1,0:T(8,128)(2,1)S(1)} copy-done((bf16[256,1024]{1,0:T(8,128)(2,1)S(1)}, bf16[256,1024]{1,0:T(8,128)(2,1)}, u32[]{:S(2)}) %copy-start.1) | copy-done | bytes 524312
  2.1 0.0 copy-start.2
  2.1 1.0 %copy-done.2 = bf16[256,1024]{1,0:T(8,128)(2,1)S(1)} copy-done((bf16[256,1024]{1,0:T(8,128)(2,1)S(1)}, bf16[256,1024]{1,0:T(8,128)(2,1)}, u32[]{:S(2)}) %copy-start.2) | copy-done | bytes 524312
  3.1 0.0 copy-start.3
  3.1 0.8 %copy-done.3 = bf16[1024,32]{0,1:T(8,128)(2,1)S(1)} copy-done((bf16[1024,32]{0,1:T(8,128)(2,1)S(1)}, bf16[1024,32]{0,1:T(8,128)(2,1)}, u32[]{:S(2)}) %copy-start.3) | copy-done | bytes 65560
  4.0 0.0 copy-start.4
  4.0 0.7 copy-done.4
  4.7 75.4 %attend_and_project.1 = bf16[1024,256]{1,0:T(8,128)(2,1)S(1)} custom-call(bf16[256,1024]{1,0:T(8,128)(2,1)S(1)} %copy-done, bf16[256,1024]{1,0:T(8,128)(2,1)S(1)} %copy-done.1, bf16[256,1024]{1,0:T(8,128)(2,1)S(1)} %copy-done.2, f32[8,128]{1,0:T(8,128)S(1)} %bitcast.5, bf16[32,1024]{1,0:T(8,128)(2,1)S(1)} %bitcast.4), custom_call_target="tpu_custom_call" | custom-call | flops 2550000128 | bytes 12000000 | tf_op jit(solution)/shard_map/attend_and_project/pallas_call | solution.py:287
  80.0 1.0 %copy.6 = bf16[256,1024]{1,0:T(8,128)(2,1)} copy(bf16[256,1024]{0,1:T(8,128)(2,1)S(1)} %bitcast.3) | data formatting | bytes 1048576 | tf_op jit(solution)/shard_map/transpose | solution.py:338
Async XLA Ops:
  0.0 1.0 %copy-start = (bf16[256,1024]{1,0:T(8,128)(2,1)S(1)}, bf16[256,1024]{1,0:T(8,128)(2,1)}, u32[]{:S(2)}) copy-start(bf16[256,1024]{1,0:T(8,128)(2,1)} %q_hbm.1) | copy-start | bytes 1572868
  1.0 1.0 %copy-start.1 = (bf16[256,1024]{1,0:T(8,128)(2,1)S(1)}, bf16[256,1024]{1,0:T(8,128)(2,1)}, u32[]{:S(2)}) copy-start(bf16[256,1024]{1,0:T(8,128)(2,1)} %k_hbm.1) | copy-start | bytes 1572868
  2.1 1.0 %copy-start.2 = (bf16[256,1024]{1,0:T(8,128)(2,1)S(1)}, bf16[256,1024]{1,0:T(8,128)(2,1)}, u32[]{:S(2)}) copy-start(bf16[256,1024]{1,0:T(8,128)(2,1)} %v_hbm.1) | copy-start | bytes 1572868
  3.1 0.8 %copy-start.3 = (bf16[1024,32]{0,1:T(8,128)(2,1)S(1)}, bf16[1024,32]{0,1:T(8,128)(2,1)}, u32[]{:S(2)}) copy-start(bf16[1024,32]{0,1:T(8,128)(2,1)} %param.9) | copy-start | bytes 196612
  4.0 0.7 copy-start.4

commit v2 on v0

v2 whole, which is shorter than its diff:
```python
import jax
import jax.numpy as jnp
from jax import lax
from jax.experimental import pallas as pl
from jax.experimental.pallas import tpu as pltpu
from jax.sharding import PartitionSpec as P

HD = 128
NY, NZ, NX = 4, 16, 4
EPS = 1e-06
MESH = pl.DeviceIdType.MESH
TICKS = 9
LAG_NEAR, LAG_FAR = 2, 4
KA = 768
LAG_PART = 2
CHUNKS = ((0, 4), (4, 4), (8, 4), (12, 3), (15, 1))
LAST_EARLY = 8


def slots(tick):
    if tick == 0:
        return 0, 1
    if tick == 8:
        return 15, 1
    return 2 * tick - 1, 2


def kernel(
    q_hbm, k_hbm, v_hbm, gain_hbm, w_hbm, out_ref,
    q_v, k_v, v_v, gain_v, q_t, within, gain_t, t_own, t_send, t_sib, c_send, z_in, pre, y_in,
    p_out, p_half, s_send, s_all, att, wa, wb, x1_send, x1_recv, x2_send, x2_recv, keep,
    load_sem, sib_sem, own_sem, once_send, once_recv, wz_recv, wl_recv, wr_recv, w2_recv, ws_recv, w_send,
    b_recv, bz_recv, bs_recv, b_send, x1_sem, x2_sem, x_send,
):
    s = lax.axis_index("seq")
    x = lax.axis_index("head")
    c = lax.rem(s, 2)
    z = lax.rem(s // 2, NZ)
    y = s // (2 * NZ)

    def at(dy=0, dz=0, dx=0, flip=False):
        yy, zz = lax.rem(y + dy + NY, NY), lax.rem(z + dz + NZ, NZ)
        return ((yy * NZ + zz) * 2 + (1 - c if flip else c), lax.rem(x + dx + NX, NX))

    def remote(src, dst, send, recv, device):
        return pltpu.make_async_remote_copy(
            src_ref=src, dst_ref=dst, send_sem=send, recv_sem=recv, device_id=device, device_id_type=MESH
        )

    def take(ref, sem):
        pltpu.make_async_copy(ref, ref, sem).wait()

    z_far = [8, 7, 9, 6, 10, 5, 11, 4, 12, 3, 13, 2, 14, 1, 15]
    barrier = pltpu.get_barrier_semaphore()
    near = [at(dz=1), at(dz=-1), at(dy=1), at(dy=2), at(dy=3), at(dx=1), at(dx=-1), at(flip=True)]
    far = [at(dz=d) for d in z_far if 1 < d < NZ - 1]

    def greet(partners):
        for partner in partners:
            pl.semaphore_signal(barrier, inc=1, device_id=partner, device_id_type=MESH)

    @pl.when(c == 0)
    def _():
        greet(far)

    greet(near)

    own_rows = pl.ds(pl.multiple_of(c * 32, 32), 32)
    loads = [
        pltpu.make_async_copy(v_hbm, v_v, load_sem.at[0]),
        pltpu.make_async_copy(k_hbm, k_v, load_sem.at[1]),
        pltpu.make_async_copy(q_hbm, q_v, load_sem.at[2]),
        pltpu.make_async_copy(gain_hbm, gain_v, load_sem.at[3]),
        pltpu.make_async_copy(w_hbm.at[:, pl.ds(0, KA)], wa.at[y, 0, own_rows], load_sem.at[4]),
        pltpu.make_async_copy(w_hbm.at[:, pl.ds(KA, wb.shape[-1])], wb.at[y, 0, own_rows], load_sem.at[5]),
    ]
    for load in loads:
        load.start()
    own_copies = [
        remote(w.at[y, 0, own_rows], w.at[y, 0, own_rows], own_sem.at[i], own_sem.at[2 + i], at(flip=True))
        for i, w in enumerate((wa, wb))
    ]

    def share_own(partners):
        loads[4].wait()
        loads[5].wait()
        pl.semaphore_wait(barrier, partners)
        for copy in own_copies:
            copy.start()

    rel = [y, lax.rem(y + NY - 1, NY), lax.rem(y + 1, NY), lax.rem(y + 2, NY)]

    part_rows = (pl.ds(32, 32), pl.ds(0, 32))

    def w_at(row, tick, part):
        first, count = slots(tick)
        return wa.at[rel[row], pl.ds(first, count), part_rows[part]]

    def to_sibling(row, tick, part):
        w = w_at(row, tick, part)
        remote(w, w, w_send.at[3 if row else 4], ws_recv.at[tick, row, part], at(flip=True)).start()

    def along_z(slot_from, slot_to, dz, part):
        rows = part_rows[part]
        remote(
            wa.at[y, slot_from, rows], wa.at[y, slot_to, rows], w_send.at[0], wz_recv.at[slot_to, part], at(dz=dz)
        ).start()

    def ring_tick(k, part):
        if k == 0:
            along_z(0, 1, 1, part)
            along_z(0, 2, -1, part)
        elif 0 < k < TICKS:
            take(wa.at[y, 2 * k - 1, part_rows[part]], wz_recv.at[2 * k - 1, part])
            if k < 8:
                along_z(2 * k - 1, 2 * k + 1, 1, part)
                take(wa.at[y, 2 * k, part_rows[part]], wz_recv.at[2 * k, part])
            if k < 7:
                along_z(2 * k, 2 * k + 2, -1, part)

    def row_tick(k, part):
        if 0 <= k < TICKS:
            w = w_at(0, k, part)
            remote(w, w, w_send.at[1], wl_recv.at[k, part], at(dy=1)).start()
            remote(w, w, w_send.at[1], wr_recv.at[k, part], at(dy=-1)).start()
            if k:
                to_sibling(0, k, part)
        j = k - LAG_NEAR
        if 0 <= j < TICKS:
            first, count = slots(j)
            take(w_at(1, j, part), wl_recv.at[j, part])
            for slot in range(first, first + count):
                if slot % 2 == 0:
                    w = wa.at[rel[1], slot, part_rows[part]]
                    remote(w, w, w_send.at[2], w2_recv.at[slot, part], at(dy=1)).start()
            to_sibling(1, j, part)
            take(w_at(2, j, part), wr_recv.at[j, part])
            for slot in range(first, first + count):
                if slot % 2 == 1:
                    w = wa.at[rel[2], slot, part_rows[part]]
                    remote(w, w, w_send.at[2], w2_recv.at[slot, part], at(dy=-1)).start()
            to_sibling(2, j, part)
        j = k - LAG_FAR
        if 0 <= j < TICKS:
            first, count = slots(j)
            for slot in range(first, first + count):
                take(wa.at[rel[3], slot, part_rows[part]], w2_recv.at[slot, part])
            to_sibling(3, j, part)

    all_rows = pl.ds(0, NY)

    def quad_start(part):
        own = wb.at[y, 0, part_rows[part]]
        for d in (1, 3, 2):
            remote(own, own, b_send.at[0], b_recv.at[part], at(dy=d)).start()

    def quad(slot_from, slot_to, dz, part):
        rows = part_rows[part]
        remote(
            wb.at[all_rows, slot_from, rows], wb.at[all_rows, slot_to, rows],
            b_send.at[1], bz_recv.at[slot_to, part], at(dz=dz),
        ).start()

    def quad_tick(k, part):
        rows = part_rows[part]
        if k == 0:
            take(wb.at[pl.ds(0, NY - 1), 0, rows], b_recv.at[part])
            quad(0, 1, 1, part)
            quad(0, 2, -1, part)
            for row in (1, 2, 3):
                w = wb.at[rel[row], 0, rows]
                remote(w, w, b_send.at[3], bs_recv.at[k, part], at(flip=True)).start()
        elif 0 < k < TICKS:
            take(wb.at[all_rows, 2 * k - 1, rows], bz_recv.at[2 * k - 1, part])
            if k < 8:
                quad(2 * k - 1, 2 * k + 1, 1, part)
                take(wb.at[all_rows, 2 * k, rows], bz_recv.at[2 * k, part])
            if k < 7:
                quad(2 * k, 2 * k + 2, -1, part)
            first, count = slots(k)
            w = wb.at[all_rows, pl.ds(first, count), rows]
            remote(w, w, b_send.at[2], bs_recv.at[k, part], at(flip=True)).start()

    def both(k):
        if k == LAG_PART:
            for copy in own_copies:
                copy.wait_recv()
        ring_tick(k, 0)
        ring_tick(k - LAG_PART, 1)
        if k == 0:
            quad_start(0)
        if k == LAG_PART:
            quad_start(1)
        quad_tick(k - 1, 0)
        quad_tick(k - LAG_PART - 1, 1)
        row_tick(k, 0)
        row_tick(k - LAG_PART, 1)

    @pl.when(c == 1)
    def _():
        share_own(len(near))
        both(0)

    loads[0].wait()
    loads[1].wait()

    heads = q_v.shape[1] // HD
    for h in range(heads):
        cols = pl.ds(h * HD, HD)
        v_t = v_v[:, cols].T
        state = jnp.dot(v_t, k_v[:, cols], preferred_element_type=jnp.float32)
        t_own[cols, :] = state
        t_send[cols, :] = state.astype(jnp.bfloat16)

    t_copy = remote(t_send, t_sib, sib_sem.at[0], sib_sem.at[1], at(flip=True))
    s_copy = remote(s_send, s_all, sib_sem.at[2], sib_sem.at[3], at(flip=True))

    before = lax.broadcasted_iota(jnp.int32, (256, 256), 0) <= lax.broadcasted_iota(jnp.int32, (256, 256), 1)

    def inside(h):
        cols = pl.ds(h * HD, HD)
        q_t[cols, :] = q_v[:, cols].T
        scores = jnp.dot(k_v[:, cols], q_t[cols, :], preferred_element_type=jnp.float32)
        scores = jnp.where(before, scores, 0.0).astype(jnp.bfloat16)
        v_t = v_v[:, cols].T
        within[cols, :] = jnp.dot(v_t, scores, preferred_element_type=jnp.float32)
        gain_t[cols, :] = jnp.broadcast_to(gain_v[h : h + 1, :], (HD, HD)).T

    half = heads // 2

    @pl.when(c == 1)
    def _():
        t_copy.start()
        both(1)

    @pl.when(c == 0)
    def _():
        share_own(len(near) + len(far))
        t_copy.wait_recv()
        c_send[...] = (t_own[...] + t_sib[...].astype(jnp.float32)).astype(jnp.bfloat16).reshape(c_send.shape)
        for d in z_far:
            remote(
                c_send.at[lax.rem(z + d, NZ)], z_in.at[z], once_send.at[0], once_recv.at[0], at(dz=d)
            ).start()
        z_in[z] = c_send[z]

    loads[2].wait()
    loads[3].wait()
    for h in range(half):
        inside(h)

    @pl.when(c == 1)
    def _():
        both(2)

    for h in range(half, heads):
        inside(h)

    @pl.when(c == 1)
    def _():
        for k in range(3, LAST_EARLY + 1):
            both(k)
        s_copy.wait_recv()

    @pl.when(c == 0)
    def _():
        take(z_in.at[pl.ds(0, NZ - 1)], once_recv.at[0])
        total = jnp.zeros(z_in.shape[1:], jnp.float32)
        for j in range(NZ):
            pre[j] = total
            total = total + z_in[j].astype(jnp.float32)
        y_in[y] = total.astype(jnp.bfloat16)
        for d in (2, 1, 3):
            remote(y_in.at[y], y_in.at[y], once_send.at[1], once_recv.at[1], at(dy=d)).start()
        take(y_in.at[pl.ds(0, NY - 1)], once_recv.at[1])
        base = jnp.zeros(z_in.shape[1:], jnp.float32)
        for j in range(NY):
            base = base + jnp.where(j < y, y_in[j].astype(jnp.float32), 0.0)
        for j in range(NZ):
            p_out[j] = (base + pre[j]).astype(jnp.bfloat16)
        for d in z_far:
            remote(
                p_out.at[lax.rem(z + d, NZ)], p_half.at[z], once_send.at[2], once_recv.at[2], at(dz=d)
            ).start()
        p_half[z] = p_out[z]
        take(p_half.at[pl.ds(0, NZ - 1)], once_recv.at[2])
        prefix = p_half[...].reshape(s_all.shape)
        s_send[...] = (prefix.astype(jnp.float32) + t_own[...]).astype(jnp.bfloat16)
        s_copy.start()
        s_all[...] = prefix
        for copy in own_copies:
            copy.wait_recv()

    for h in range(heads):
        cols = pl.ds(h * HD, HD)
        combined = within[cols, :] + jnp.dot(s_all[cols, :], q_t[cols, :], preferred_element_type=jnp.float32)
        mean = jnp.mean(combined * combined, axis=0, keepdims=True)
        att[cols, :] = (combined * lax.rsqrt(mean + EPS) * gain_t[cols, 0:1]).astype(jnp.bfloat16)

    right, left, across = lax.rem(x + 1, NX), lax.rem(x + NX - 1, NX), lax.rem(x + 2, NX)

    def partial(dest, g):
        first, count = CHUNKS[g]
        a = wa[dest, first : first + count].reshape(64 * count, KA)
        b = wb[dest, first : first + count].reshape(64 * count, wb.shape[-1])
        return jnp.dot(a, att[:KA, :], preferred_element_type=jnp.float32) + jnp.dot(
            b, att[KA:, :], preferred_element_type=jnp.float32
        )

    def x_rows(g):
        first, count = CHUNKS[g]
        return pl.ds(32 * first, 32 * count), 32 * count

    def x2_start(g, way, part, dx):
        rows, _ = x_rows(g)
        remote(
            x2_send.at[way, part, rows], x2_recv.at[way, part, rows], x_send.at[1], x2_sem.at[g, way, part], at(dx=dx)
        ).start()

    def last_tick(g):
        return (CHUNKS[g][0] + CHUNKS[g][1]) // 2

    def arrived(g):
        for t in range(last_tick(g - 1) + 1 if g else 0, last_tick(g) + 1):
            first, count = slots(t)
            for part, rows in enumerate(part_rows):
                take(wb.at[pl.ds(0, NY if t else NY - 1), pl.ds(first, count), rows], bs_recv.at[t, part])
                for row in range(0 if t else 1, 4):
                    take(w_at(row, t, part), ws_recv.at[t, row, part])

    def project(g):
        rows, half_rows = x_rows(g)
        opposite = partial(across, g).astype(jnp.bfloat16)
        for way, dx in ((0, 1), (1, -1)):
            x1_send[way, rows] = opposite[way * half_rows : (way + 1) * half_rows]
            remote(
                x1_send.at[way, rows], x1_recv.at[way, rows], x_send.at[0], x1_sem.at[g, way], at(dx=dx)
            ).start()
        near = partial(right, g)
        x2_send[0, 1, rows] = near[half_rows:].astype(jnp.bfloat16)
        x2_start(g, 0, 1, 1)
        keep[0, rows] = near[:half_rows]
        near = partial(left, g)
        x2_send[1, 0, rows] = near[:half_rows].astype(jnp.bfloat16)
        x2_start(g, 1, 0, -1)
        keep[1, rows] = near[half_rows:]
        own = partial(x, g)
        keep[2, rows] = own[:half_rows]
        keep[3, rows] = own[half_rows:]

    def join(g):
        rows, _ = x_rows(g)
        for way, dx in ((0, 1), (1, -1)):
            take(x1_recv.at[way, rows], x1_sem.at[g, way])
            x2_send[way, way, rows] = (keep[way, rows] + x1_recv[way, rows].astype(jnp.float32)).astype(jnp.bfloat16)
            x2_start(g, way, way, dx)

    def finish(g):
        rows, half_rows = x_rows(g)
        for way, part in ((0, 1), (1, 0), (0, 0), (1, 1)):
            take(x2_recv.at[way, part, rows], x2_sem.at[g, way, part])
        for part in range(2):
            total = keep[2 + part, rows] + (
                x2_recv[0, part, rows].astype(jnp.float32) + x2_recv[1, part, rows].astype(jnp.float32)
            )
            total = total.astype(jnp.bfloat16)
            for i in range(half_rows // 32):
                unit = 2 * CHUNKS[g][0] + part * (half_rows // 32) + i
                slot, core = unit // 2, unit % 2
                step = (slot + 1) // 2
                where = lax.rem(z + (NZ - step if slot % 2 == 1 else step), NZ)
                out_ref[pl.ds(pl.multiple_of(where * 64 + core * 32, 32), 32), :] = total[32 * i : 32 * i + 32]

    done = LAST_EARLY
    count = len(CHUNKS)
    for g in range(count):
        need = max(done, last_tick(g) + LAG_PART + LAG_FAR)

        @pl.when(c == 1)
        def _():
            for k in range(done + 1, need + 1):
                both(k)

        @pl.when(c == 0)
        def _():
            arrived(g)

        done = need
        project(g)
        if g >= 1:
            join(g - 1)
        if g >= 2:
            finish(g - 2)
    join(count - 1)
    finish(count - 2)
    finish(count - 1)

    for copy in own_copies:
        copy.wait_send()
    take(x1_recv, x_send.at[0])
    take(x2_recv, x_send.at[1])

    @pl.when(c == 0)
    def _():
        s_copy.wait_send()
        take(z_in.at[pl.ds(0, NZ - 1)], once_send.at[0])
        take(y_in.at[pl.ds(0, NY - 1)], once_send.at[1])
        take(p_half.at[pl.ds(0, NZ - 1)], once_send.at[2])

    @pl.when(c == 1)
    def _():
        t_copy.wait_send()
        take(wa.at[0, pl.ds(0, 15)], w_send.at[0])
        take(wa.at[pl.ds(0, 2)], w_send.at[1])
        take(wa.at[0], w_send.at[2])
        take(wa.at[pl.ds(0, 3)], w_send.at[3])
        take(wa.at[0, pl.ds(0, 15)], w_send.at[4])
        take(wb.at[pl.ds(0, NY - 1), 0], b_send.at[0])
        take(wb.at[:, pl.ds(0, 15)], b_send.at[1])
        take(wb.at[pl.ds(0, NY - 1), 0], b_send.at[3])
        take(wb.at[:, pl.ds(0, 15)], b_send.at[2])


def body(queries, key_vectors, value_vectors, norm_gain, out_weight):
    tokens, features = queries.shape
    heads = features // HD
    bf16, f32 = jnp.bfloat16, jnp.float32
    sem = pltpu.SemaphoreType.DMA
    anywhere = pl.BlockSpec(memory_space=pl.ANY)
    out = pl.pallas_call(
        kernel,
        out_shape=jax.ShapeDtypeStruct((features, tokens), bf16),
        in_specs=[anywhere] * 5,
        out_specs=pl.BlockSpec(memory_space=pltpu.VMEM),
        scratch_shapes=[
            pltpu.VMEM((tokens, features), bf16),
            pltpu.VMEM((tokens, features), bf16),
            pltpu.VMEM((tokens, features), bf16),
            pltpu.VMEM((heads, HD), f32),
            pltpu.VMEM((features, tokens), bf16),
            pltpu.VMEM((features, tokens), f32),
            pltpu.VMEM((features, HD), f32),
            pltpu.VMEM((features, HD), f32),
            pltpu.VMEM((features, HD), bf16),
            pltpu.VMEM((features, HD), bf16),
            pltpu.VMEM((NZ, features // NZ, HD), bf16),
            pltpu.VMEM((NZ, features // NZ, HD), bf16),
            pltpu.VMEM((NZ, features // NZ, HD), f32),
            pltpu.VMEM((NY, features // NZ, HD), bf16),
            pltpu.VMEM((NZ, features // NZ, HD), bf16),
            pltpu.VMEM((NZ, features // NZ, HD), bf16),
            pltpu.VMEM((features, HD), bf16),
            pltpu.VMEM((features, HD), bf16),
            pltpu.VMEM((features, tokens), bf16),
            pltpu.VMEM((NY, NZ, 64, KA), bf16),
            pltpu.VMEM((NY, NZ, 64, features - KA), bf16),
            pltpu.VMEM((2, features // 2, tokens), bf16),
            pltpu.VMEM((2, features // 2, tokens), bf16),
            pltpu.VMEM((2, 2, features // 2, tokens), bf16),
            pltpu.VMEM((2, 2, features // 2, tokens), bf16),
            pltpu.VMEM((4, features // 2, tokens), f32),
            sem((6,)),
            sem((4,)),
            sem((4,)),
            sem((3,)),
            sem((3,)),
            sem((16, 2)),
            sem((TICKS, 2)),
            sem((TICKS, 2)),
            sem((16, 2)),
            sem((TICKS, 4, 2)),
            sem((5,)),
            sem((2,)),
            sem((16, 2)),
            sem((TICKS, 2)),
            sem((4,)),
            sem((len(CHUNKS), 2)),
            sem((len(CHUNKS), 2, 2)),
            sem((2,)),
        ],
        compiler_params=pltpu.CompilerParams(
            collective_id=0, has_side_effects=True, vmem_limit_bytes=62 << 20
        ),
        cost_estimate=pl.CostEstimate(flops=2_550_000_000, bytes_accessed=12_000_000, transcendentals=4096),
        name="attend_and_project",
    )(queries, key_vectors, value_vectors, norm_gain.reshape(heads, HD), out_weight.T)
    return out.T


def solution(mesh):
    in_specs = (P("seq", "head"), P("seq", "head"), P("seq", "head"), P("head"), P("head", "seq"))
    return jax.shard_map(body, mesh=mesh, in_specs=in_specs, out_specs=P("seq", "head"), check_vma=False)
```

time: 408 us -> 76.9 us (0.19)
  waiting for transfers between devices: 376 us -> 0 us
  Pallas kernels: 0 us -> 73.9 us
  between operations: 13.2 us -> 0.01 us
  matrix products: 11.4 us -> 0 us
    all_gather x2 -> x0, waiting for transfers between devices: 344 us -> none  [the longest x1 201 us: carried_in(): gathered = lax.all_gather(shard.astype(jnp.bfloat16), axis)]
    pallas_call x0 -> x1, Pallas kernels: none -> 73.9 us  [body(): pl.pallas_call(kernel, out_shape=jax.ShapeDtypeStruct((features, tokens),...]
    reduce_scatter x1 -> x0, waiting for transfers between devices: 32.2 us -> none  [body(): lax.psum_scatter(partial_sums.astype(jnp.bfloat16), 'head', scatter_dimen...]
    dot_general x4 -> x0, matrix products: 11.4 us -> none  [the longest x1 7.19 us: body(): jnp.dot(attended, full_weight, preferred_element_type=jnp.float32)]
  transfers between devices with their start and end apart: 3 -> 0, of which waited for: 3 -> 0; matrix products, arithmetic and copies ran while one was open for 1% -> 0% of each run, Pallas kernels for 0% -> 0%
where the time goes in v2:
time: 76.9 us; the launch traced here: 75.9 us
  Pallas kernels  73.9 us (96%)
  local copies, waits for them, and re-layouts  2.04 us (3%)
    pallas_call x1, Pallas kernels, body(): pl.pallas_call(kernel, out_shape=jax.ShapeDtypeStruct((features, tokens),...  73.9 us
    transpose x1, local copies, waits for them, and re-layouts, body(): return out.T  2.04 us

profile of v2, /device:TPU:1, one launch (start us, length us, event | category | flops | bytes accessed | tf_op | source)
XLA Modules:
  0.0 75.9 jit_solution(4438094275950243502)
XLA Ops:
  0.0 73.9 %attend_and_project.1 = bf16[1024,256]{1,0:T(8,128)(2,1)} custom-call(bf16[256,1024]{1,0:T(8,128)(2,1)} %q_hbm.1, bf16[256,1024]{1,0:T(8,128)(2,1)} %k_hbm.1, bf16[256,1024]{1,0:T(8,128)(2,1)} %v_hbm.1, f32[8,128]{1,0:T(8,128)} %bitcast.5, bf16[32,1024]{1,0:T(8,128)(2,1)} %bitcast.4), custom_call_target="tpu_custom_call" | custom-call | flops 2550000128 | bytes 12000000 | tf_op jit(solution)/shard_map/attend_and_project/pallas_call | solution.py:430
  73.9 2.0 %copy.6 = bf16[256,1024]{1,0:T(8,128)(2,1)} copy(bf16[256,1024]{0,1:T(8,128)(2,1)} %bitcast.3) | data formatting | bytes 1048576 | tf_op jit(solution)/shard_map/transpose | solution.py:487

commit v3 on v2

--- a/solution.py
+++ b/solution.py
@@ -9,12 +9,14 @@
 NY, NZ, NX = 4, 16, 4
 EPS = 1e-06
 MESH = pl.DeviceIdType.MESH
+PAIRS = NZ // 2
 TICKS = 9
 LAG_NEAR, LAG_FAR = 2, 4
 KA = 768
 LAG_PART = 2
+LONG_WAY = 1
 CHUNKS = ((0, 4), (4, 4), (8, 4), (12, 3), (15, 1))
-LAST_EARLY = 8
+LAST_EARLY = 10
 
 
 def slots(tick):
@@ -27,9 +29,9 @@
 
 def kernel(
     q_hbm, k_hbm, v_hbm, gain_hbm, w_hbm, out_ref,
-    q_v, k_v, v_v, gain_v, q_t, within, gain_t, t_own, t_send, t_sib, c_send, z_in, pre, y_in,
-    p_out, p_half, s_send, s_all, att, wa, wb, x1_send, x1_recv, x2_send, x2_recv, keep,
-    load_sem, sib_sem, own_sem, once_send, once_recv, wz_recv, wl_recv, wr_recv, w2_recv, ws_recv, w_send,
+    q_v, k_v, v_v, gain_v, q_t, within, gain_t, t_own, t_send, t_sib, chip, pair_send, pair_in, back_send, s_pre, c_send, z_in, pre, y_in,
+    p_out, p_half, s_send, s_all, att, wa, wb, x1_send, x1_recv, x2_send, x2_recv, keep, out_t,
+    load_sem, sib_sem, own_sem, pair_sem, once_send, once_recv, wz_recv, wl_recv, wr_recv, w2_recv, ws_recv, w_send,
     b_recv, bz_recv, bs_recv, b_send, x1_sem, x2_sem, x_send,
 ):
     s = lax.axis_index("seq")
@@ -50,10 +52,10 @@
     def take(ref, sem):
         pltpu.make_async_copy(ref, ref, sem).wait()
 
-    z_far = [8, 7, 9, 6, 10, 5, 11, 4, 12, 3, 13, 2, 14, 1, 15]
+    pair_far = [8, 6, 10, 4, 12, 2, 14]
     barrier = pltpu.get_barrier_semaphore()
     near = [at(dz=1), at(dz=-1), at(dy=1), at(dy=2), at(dy=3), at(dx=1), at(dx=-1), at(flip=True)]
-    far = [at(dz=d) for d in z_far if 1 < d < NZ - 1]
+    far = [at(dz=d) for d in pair_far]
 
     def greet(partners):
         for partner in partners:
@@ -103,7 +105,7 @@
     def along_z(slot_from, slot_to, dz, part):
         rows = part_rows[part]
         remote(
-            wa.at[y, slot_from, rows], wa.at[y, slot_to, rows], w_send.at[0], wz_recv.at[slot_to, part], at(dz=dz)
+            wa.at[y, slot_from, rows], wa.at[y, slot_to, rows], w_send.at[0], wz_recv.at[slot_to, part], at(dz=dz * LONG_WAY)
         ).start()
 
     def ring_tick(k, part):
@@ -158,7 +160,7 @@
         rows = part_rows[part]
         remote(
             wb.at[all_rows, slot_from, rows], wb.at[all_rows, slot_to, rows],
-            b_send.at[1], bz_recv.at[slot_to, part], at(dz=dz),
+            b_send.at[1], bz_recv.at[slot_to, part], at(dz=dz * LONG_WAY),
         ).start()
 
     def quad_tick(k, part):
@@ -213,6 +215,13 @@
         t_send[cols, :] = state.astype(jnp.bfloat16)
 
     t_copy = remote(t_send, t_sib, sib_sem.at[0], sib_sem.at[1], at(flip=True))
+    pair, second = z // 2, lax.rem(z, 2)
+    rows_half = t_own.shape[0] // 2
+    mine = pl.ds(pl.multiple_of(second * rows_half, rows_half), rows_half)
+    theirs = pl.ds(pl.multiple_of((1 - second) * rows_half, rows_half), rows_half)
+    neighbour = at(dz=1 - 2 * second)
+    pair_copy = remote(pair_send, pair_in, pair_sem.at[0], pair_sem.at[1], neighbour)
+    back_copy = remote(back_send, s_pre.at[mine], pair_sem.at[2], pair_sem.at[3], neighbour)
     s_copy = remote(s_send, s_all, sib_sem.at[2], sib_sem.at[3], at(flip=True))
 
     before = lax.broadcasted_iota(jnp.int32, (256, 256), 0) <= lax.broadcasted_iota(jnp.int32, (256, 256), 1)
@@ -237,12 +246,17 @@
     def _():
         share_own(len(near) + len(far))
         t_copy.wait_recv()
-        c_send[...] = (t_own[...] + t_sib[...].astype(jnp.float32)).astype(jnp.bfloat16).reshape(c_send.shape)
-        for d in z_far:
+        chip[...] = t_own[...] + t_sib[...].astype(jnp.float32)
+        pair_send[...] = chip[theirs, :].astype(jnp.bfloat16)
+        pair_copy.start()
+        pair_copy.wait_recv()
+        both_chips = chip[mine, :] + pair_in[...].astype(jnp.float32)
+        c_send[...] = both_chips.astype(jnp.bfloat16).reshape(c_send.shape)
+        for d in pair_far:
             remote(
-                c_send.at[lax.rem(z + d, NZ)], z_in.at[z], once_send.at[0], once_recv.at[0], at(dz=d)
+                c_send.at[lax.rem(pair + d // 2, PAIRS)], z_in.at[pair], once_send.at[0], once_recv.at[0], at(dz=d)
             ).start()
-        z_in[z] = c_send[z]
+        z_in[pair] = c_send[pair]
 
     loads[2].wait()
     loads[3].wait()
@@ -264,9 +278,9 @@
 
     @pl.when(c == 0)
     def _():
-        take(z_in.at[pl.ds(0, NZ - 1)], once_recv.at[0])
+        take(z_in.at[pl.ds(0, PAIRS - 1)], once_recv.at[0])
         total = jnp.zeros(z_in.shape[1:], jnp.float32)
-        for j in range(NZ):
+        for j in range(PAIRS):
             pre[j] = total
             total = total + z_in[j].astype(jnp.float32)
         y_in[y] = total.astype(jnp.bfloat16)
@@ -276,15 +290,22 @@
         base = jnp.zeros(z_in.shape[1:], jnp.float32)
         for j in range(NY):
             base = base + jnp.where(j < y, y_in[j].astype(jnp.float32), 0.0)
-        for j in range(NZ):
+        for j in range(PAIRS):
             p_out[j] = (base + pre[j]).astype(jnp.bfloat16)
-        for d in z_far:
+        for d in pair_far:
             remote(
-                p_out.at[lax.rem(z + d, NZ)], p_half.at[z], once_send.at[2], once_recv.at[2], at(dz=d)
+                p_out.at[lax.rem(pair + d // 2, PAIRS)], p_half.at[pair], once_send.at[2], once_recv.at[2], at(dz=d)
             ).start()
-        p_half[z] = p_out[z]
-        take(p_half.at[pl.ds(0, NZ - 1)], once_recv.at[2])
-        prefix = p_half[...].reshape(s_all.shape)
+        p_half[pair] = p_out[pair]
+        take(p_half.at[pl.ds(0, PAIRS - 1)], once_recv.at[2])
+        before_pair = p_half[...].reshape(pair_in.shape).astype(jnp.float32)
+        back_send[...] = (before_pair + jnp.where(second == 0, chip[mine, :], 0.0)).astype(jnp.bfloat16)
+        back_copy.start()
+        s_pre[mine, :] = (
+            before_pair + jnp.where(second == 1, pair_in[...].astype(jnp.float32), 0.0)
+        ).astype(jnp.bfloat16)
+        back_copy.wait_recv()
+        prefix = s_pre[...]
         s_send[...] = (prefix.astype(jnp.float32) + t_own[...]).astype(jnp.bfloat16)
         s_copy.start()
         s_all[...] = prefix
@@ -368,8 +389,8 @@
                 unit = 2 * CHUNKS[g][0] + part * (half_rows // 32) + i
                 slot, core = unit // 2, unit % 2
                 step = (slot + 1) // 2
-                where = lax.rem(z + (NZ - step if slot % 2 == 1 else step), NZ)
-                out_ref[pl.ds(pl.multiple_of(where * 64 + core * 32, 32), 32), :] = total[32 * i : 32 * i + 32]
+                where = lax.rem(z + NZ + (-step if slot % 2 == 1 else step) * LONG_WAY, NZ)
+                out_t[pl.ds(pl.multiple_of(where * 64 + core * 32, 32), 32), :] = total[32 * i : 32 * i + 32]
 
     done = LAST_EARLY
     count = len(CHUNKS)
@@ -394,6 +415,7 @@
     join(count - 1)
     finish(count - 2)
     finish(count - 1)
+    out_ref[...] = out_t[...].T
 
     for copy in own_copies:
         copy.wait_send()
@@ -403,9 +425,11 @@
     @pl.when(c == 0)
     def _():
         s_copy.wait_send()
-        take(z_in.at[pl.ds(0, NZ - 1)], once_send.at[0])
+        pair_copy.wait_send()
+        back_copy.wait_send()
+        take(z_in.at[pl.ds(0, PAIRS - 1)], once_send.at[0])
         take(y_in.at[pl.ds(0, NY - 1)], once_send.at[1])
-        take(p_half.at[pl.ds(0, NZ - 1)], once_send.at[2])
+        take(p_half.at[pl.ds(0, PAIRS - 1)], once_send.at[2])
 
     @pl.when(c == 1)
     def _():
@@ -427,9 +451,9 @@
     bf16, f32 = jnp.bfloat16, jnp.float32
     sem = pltpu.SemaphoreType.DMA
     anywhere = pl.BlockSpec(memory_space=pl.ANY)
-    out = pl.pallas_call(
+    return pl.pallas_call(
         kernel,
-        out_shape=jax.ShapeDtypeStruct((features, tokens), bf16),
+        out_shape=jax.ShapeDtypeStruct((tokens, features), bf16),
         in_specs=[anywhere] * 5,
         out_specs=pl.BlockSpec(memory_space=pltpu.VMEM),
         scratch_shapes=[
@@ -443,12 +467,17 @@
             pltpu.VMEM((features, HD), f32),
             pltpu.VMEM((features, HD), bf16),
             pltpu.VMEM((features, HD), bf16),
-            pltpu.VMEM((NZ, features // NZ, HD), bf16),
-            pltpu.VMEM((NZ, features // NZ, HD), bf16),
-            pltpu.VMEM((NZ, features // NZ, HD), f32),
+            pltpu.VMEM((features, HD), f32),
+            pltpu.VMEM((features // 2, HD), bf16),
+            pltpu.VMEM((features // 2, HD), bf16),
+            pltpu.VMEM((features // 2, HD), bf16),
+            pltpu.VMEM((features, HD), bf16),
+            pltpu.VMEM((PAIRS, features // NZ, HD), bf16),
+            pltpu.VMEM((PAIRS, features // NZ, HD), bf16),
+            pltpu.VMEM((PAIRS, features // NZ, HD), f32),
             pltpu.VMEM((NY, features // NZ, HD), bf16),
-            pltpu.VMEM((NZ, features // NZ, HD), bf16),
-            pltpu.VMEM((NZ, features // NZ, HD), bf16),
+            pltpu.VMEM((PAIRS, features // NZ, HD), bf16),
+            pltpu.VMEM((PAIRS, features // NZ, HD), bf16),
             pltpu.VMEM((features, HD), bf16),
             pltpu.VMEM((features, HD), bf16),
             pltpu.VMEM((features, tokens), bf16),
@@ -459,7 +488,9 @@
             pltpu.VMEM((2, 2, features // 2, tokens), bf16),
             pltpu.VMEM((2, 2, features // 2, tokens), bf16),
             pltpu.VMEM((4, features // 2, tokens), f32),
+            pltpu.VMEM((features, tokens), bf16),
             sem((6,)),
+            sem((4,)),
             sem((4,)),
             sem((4,)),
             sem((3,)),
@@ -484,7 +515,6 @@
         cost_estimate=pl.CostEstimate(flops=2_550_000_000, bytes_accessed=12_000_000, transcendentals=4096),
         name="attend_and_project",
     )(queries, key_vectors, value_vectors, norm_gain.reshape(heads, HD), out_weight.T)
-    return out.T
 
 
 def solution(mesh):

time: 76.9 us -> 74.1 us (0.964)
  the two profiles are of different devices: /device:TPU:1 before, /device:TPU:32 now
where the time goes in v3:
time: 74.1 us; the launch traced here: 73.9 us
  Pallas kernels  72 us (97%)
  local copies, waits for them, and re-layouts  1.87 us (3%)
    pallas_call x1, Pallas kernels, body(): pl.pallas_call(kernel, out_shape=jax.ShapeDtypeStruct((tokens, features),...  72 us
    unnamed x1, local copies, waits for them, and re-layouts  1.87 us

profile of v3, /device:TPU:32, one launch (start us, length us, event | category | flops | bytes accessed | tf_op | source)
XLA Modules:
  0.0 73.9 jit_solution(8288678214073897353)
XLA Ops:
  0.0 72.0 %attend_and_project.1 = bf16[256,1024]{1,0:T(8,128)(2,1)} custom-call(bf16[256,1024]{1,0:T(8,128)(2,1)} %q_hbm.1, bf16[256,1024]{1,0:T(8,128)(2,1)} %k_hbm.1, bf16[256,1024]{1,0:T(8,128)(2,1)} %v_hbm.1, f32[8,128]{1,0:T(8,128)} %bitcast.3, bf16[32,1024]{1,0:T(8,128)(2,1)} %bitcast.2), custom_call_target="tpu_custom_call" | custom-call | flops 2550000128 | bytes 12000000 | tf_op jit(solution)/shard_map/attend_and_project/pallas_call | solution.py:454
  72.0 1.9 %copy.7 = bf16[256,1024]{1,0:T(8,128)(2,1)} copy(bf16[256,1024]{1,0:T(8,128)(2,1)} %attend_and_project.1) | data formatting | bytes 1048576

commit v4 on v3

--- a/solution.py
+++ b/solution.py
@@ -12,7 +12,7 @@
 PAIRS = NZ // 2
 TICKS = 9
 LAG_NEAR, LAG_FAR = 2, 4
-KA = 768
+KA = 896
 LAG_PART = 2
 LONG_WAY = 1
 CHUNKS = ((0, 4), (4, 4), (8, 4), (12, 3), (15, 1))

time: 74.1 us -> 74.5 us (level)
  the two profiles are of different devices: /device:TPU:32 before, /device:TPU:1 now
where the time goes in v4:
time: 74.5 us; the launch traced here: 73.7 us
  Pallas kernels  71.8 us (96%)
  local copies, waits for them, and re-layouts  1.87 us (3%)
    pallas_call x1, Pallas kernels, body(): pl.pallas_call(kernel, out_shape=jax.ShapeDtypeStruct((tokens, features),...  71.8 us
    unnamed x1, local copies, waits for them, and re-layouts  1.87 us

profile of v4, /device:TPU:1, one launch (start us, length us, event | category | flops | bytes accessed | tf_op | source)
XLA Modules:
  0.0 73.7 jit_solution(16362050691737356397)
XLA Ops:
  0.0 71.8 %attend_and_project.1 = bf16[256,1024]{1,0:T(8,128)(2,1)} custom-call(bf16[256,1024]{1,0:T(8,128)(2,1)} %q_hbm.1, bf16[256,1024]{1,0:T(8,128)(2,1)} %k_hbm.1, bf16[256,1024]{1,0:T(8,128)(2,1)} %v_hbm.1, f32[8,128]{1,0:T(8,128)} %bitcast.3, bf16[32,1024]{1,0:T(8,128)(2,1)} %bitcast.2), custom_call_target="tpu_custom_call" | custom-call | flops 2550000128 | bytes 12000000 | tf_op jit(solution)/shard_map/attend_and_project/pallas_call | solution.py:454
  71.8 1.9 %copy.7 = bf16[256,1024]{1,0:T(8,128)(2,1)} copy(bf16[256,1024]{1,0:T(8,128)(2,1)} %attend_and_project.1) | data formatting | bytes 1048576
